TPU v7x, 32 devices: a whole 2x2x4 slice. The times are simulated.
32 devices in a mesh: batch: 2 (over y), fx: 4 (over z), fy: 4 (over x, core).
Axes of the slice: x: 2, y: 2, z: 4, core: 2. Of those that a mesh axis runs over, the one named last changes fastest.
Arguments:
- image_pool: bfloat16 [2, 4, 256, 6144], P('batch', None, None, 'fx'), may hold values from -6 to 6
- escalated: int32 [2, 2], P('batch'), may hold values from 0 to 3
- up_weight: bfloat16 [6144, 24576], P('fx', 'fy'), may hold values from -0.078125 to 0.078125
- down_weight: bfloat16 [24576, 6144], P('fy', 'fx'), may hold values from -0.0390625 to 0.0390625
- cotangent: bfloat16 [2, 2, 256, 6144], P('batch', None, None, 'fx'), may hold values from -6 to 6
Outputs:
- input_grad: bfloat16 [2, 2, 256, 6144], P('batch', None, None, 'fx')
- up_grad: bfloat16 [6144, 24576], P('fx', 'fy')
- down_grad: bfloat16 [24576, 6144], P('fy', 'fx')
All inputs are finite; a program needn't handle non-finite values.
Results may differ from a plain program's by a relative error of at most 0.018.
Values may be sent and summed in bfloat16 or wider, within the bound.
A program may use at most 256 MiB of HBM per device.

v0:
```python
import jax
import jax.numpy as jnp
from jax import lax
from jax.sharding import PartitionSpec as P

root_half = 0.7071067811865476
inv_root_tau = 0.3989422804014327


def gelu_value(pre_act):
    return 0.5 * pre_act * (1.0 + lax.erf(pre_act * root_half))


def gelu_slope(pre_act):
    return (
        0.5 * (1.0 + lax.erf(pre_act * root_half))
        + pre_act * jnp.exp(-0.5 * pre_act * pre_act) * inv_root_tau
    )


def contract_rows(left, right):
    return lax.dot_general(
        left, right, (((0,), (0,)), ((), ())), preferred_element_type=jnp.float32
    )


def per_device(image_pool, escalated, up_weight, down_weight, cotangent):
    fx_width = image_pool.shape[3]
    chosen = jnp.take(image_pool[0], escalated[0], axis=0)
    inputs = chosen.reshape(-1, fx_width)
    upstream = cotangent.reshape(-1, fx_width)
    pre_part = jnp.dot(inputs, up_weight, preferred_element_type=jnp.float32)
    back_part = lax.dot_general(
        upstream, down_weight, (((1,), (1,)), ((), ())), preferred_element_type=jnp.float32
    )
    pre_act, grad_act = (
        lax.psum_scatter(
            pre_part.astype(jnp.bfloat16), "fx", scatter_dimension=0, tiled=True
        ).astype(jnp.float32),
        lax.psum_scatter(
            back_part.astype(jnp.bfloat16), "fx", scatter_dimension=0, tiled=True
        ).astype(jnp.float32),
    )
    act_share = gelu_value(pre_act).astype(jnp.bfloat16)
    grad_share = (grad_act * gelu_slope(pre_act)).astype(jnp.bfloat16)
    act_rows, grad_rows = (
        lax.all_gather(act_share, "fx", axis=0, tiled=True),
        lax.all_gather(grad_share, "fx", axis=0, tiled=True),
    )
    input_part = lax.dot_general(
        grad_rows, up_weight, (((1,), (1,)), ((), ())), preferred_element_type=jnp.float32
    )
    input_total = lax.psum(input_part.astype(jnp.bfloat16), "fy")
    input_grad = input_total.reshape(cotangent.shape)
    up_tile = contract_rows(inputs, grad_rows)
    down_tile = contract_rows(act_rows, upstream)
    up_total, down_total = (
        lax.psum(up_tile.astype(jnp.bfloat16), "batch").astype(jnp.float32),
        lax.psum(down_tile.astype(jnp.bfloat16), "batch").astype(jnp.float32),
    )
    return (input_grad, up_total.astype(jnp.bfloat16), down_total.astype(jnp.bfloat16))


def solution(mesh):
    placed = (
        P("batch", None, None, "fx"),
        P("batch", None),
        P("fx", "fy"),
        P("fy", "fx"),
        P("batch", None, None, "fx"),
    )
    return jax.shard_map(
        per_device,
        mesh=mesh,
        in_specs=placed,
        out_specs=(P("batch", None, None, "fx"), P("fx", "fy"), P("fy", "fx")),
        check_vma=False,
    )
```

profile of v0, /device:TPU:0, one launch (start us, length us, event | category | flops | bytes accessed | tf_op | source)
XLA Modules:
  0.0 1403.7 jit_solution(12932830395947247648)
XLA Ops:
  7.2 0.0 reduce-scatter.5.cloned.1.call-start
  7.2 0.8 fusion.9
  8.0 0.8 compare_and_fusion
  8.8 0.1 broadcast_in_dim.14
  8.9 0.2 copy-done
  9.1 1.8 gather_fusion
  10.9 1.6 bitcast_select_fusion
  12.5 15.5 %convolution_convert_fusion.2 = bf16[512,6144]{1,0:T(8,128)(2,1)} fusion(bf16[512,1536]{1,0:T(8,128)(2,1)S(1)} %bitcast_select_fusion, bf16[1536,6144]{1,0:T(8,128)(2,1)} %param.7), kind=kOutput, calls=%fused_computation.3 | convolution fusion | flops 9666822144 | bytes 26738688 | tf_op jit(solution)/shard_map/dot_general | solution.py:32
  27.9 0.0 reduce-scatter.5.cloned.1.call-update
  28.0 0.0 reduce-scatter.3.cloned.1.call-start
  28.0 1.3 copy-done.2
  29.3 15.5 %convolution_convert_fusion.3 = bf16[512,6144]{1,0:T(8,128)(2,1)} fusion(bf16[512,1536]{1,0:T(8,128)(2,1)S(1)} %bitcast.25, bf16[6144,1536]{1,0:T(8,128)(2,1)} %param.8), kind=kOutput, calls=%fused_computation.4 | convolution fusion | flops 9666822144 | bytes 26738688 | tf_op jit(solution)/shard_map/dot_general | solution.py:33
  44.8 0.0 reduce-scatter.3.cloned.1.call-update
  44.9 0.0 all-gather.3.cloned.1.call-start
  44.9 96.7 %reduce-scatter.5.cloned.1.call-done = bf16[128,6144]{1,0:T(8,128)(2,1)} async-done(((bf16[512,6144]{1,0:T(8,128)(2,1)}), bf16[128,6144]{1,0:T(8,128)(2,1)}) %reduce-scatter.5.cloned.1.call-update) | async-done | bytes 1572880 | tf_op jit(solution)/shard_map/reduce_scatter | solution.py:37
  141.6 114.2 %reduce-scatter.3.cloned.1.call-done = bf16[128,6144]{1,0:T(8,128)(2,1)} async-done(((bf16[512,6144]{1,0:T(8,128)(2,1)}), bf16[128,6144]{1,0:T(8,128)(2,1)}) %reduce-scatter.3.cloned.1.call-update) | async-done | bytes 1572880 | tf_op jit(solution)/shard_map/reduce_scatter | solution.py:40
  255.7 4.3 fusion.8
  260.0 0.0 all-gather.3.cloned.1.call-update
  260.0 0.0 all-gather.5.cloned.1.call-start
  260.1 0.5 all-gather.5.cloned.1.call-update
  260.6 0.2 all-reduce.4.cloned.1.call-start
  260.8 115.2 %all-gather.3.cloned.1.call-done = bf16[512,6144]{1,0:T(8,128)(2,1)} async-done(((bf16[128,6144]{1,0:T(8,128)(2,1)}), bf16[512,6144]{1,0:T(8,128)(2,1)}) %all-gather.3.cloned.1.call-update) | async-done | bytes 6291472 | tf_op jit(solution)/shard_map/all_gather | solution.py:48
  376.1 16.5 %convolution_convert_fusion.4 = bf16[512,1536]{1,0:T(8,128)(2,1)} fusion(bf16[512,6144]{1,0:T(8,128)(2,1)} %all-gather.3.cloned.1.call-done, bf16[1536,6144]{1,0:T(8,128)(2,1)} %param.7), kind=kOutput, calls=%fused_computation.19 | convolution fusion | flops 9664462848 | bytes 26738688 | tf_op jit(solution)/shard_map/dot_general | solution.py:50
  392.6 0.0 all-reduce.6.cloned.1.call-start
  392.7 99.0 %all-gather.5.cloned.1.call-done = bf16[512,6144]{1,0:T(8,128)(2,1)} async-done(((bf16[128,6144]{1,0:T(8,128)(2,1)}), bf16[512,6144]{1,0:T(8,128)(2,1)}) %all-gather.5.cloned.1.call-update) | async-done | bytes 6291472 | tf_op jit(solution)/shard_map/all_gather | solution.py:47
  491.7 15.9 %convolution_convert_fusion.1 = bf16[6144,1536]{1,0:T(8,128)(2,1)} fusion(bf16[512,6144]{1,0:T(8,128)(2,1)} %all-gather.5.cloned.1.call-done, bf16[512,1536]{1,0:T(8,128)(2,1)S(1)} %bitcast.26), kind=kOutput, calls=%fused_computation.2 | convolution fusion | flops 9673113600 | bytes 26738688 | tf_op jit(solution)/shard_map/dot_general | solution.py:22
  507.6 15.9 %convolution_convert_fusion = bf16[1536,6144]{1,0:T(8,128)(2,1)} fusion(bf16[512,1536]{1,0:T(8,128)(2,1)S(1)} %bitcast_select_fusion, bf16[512,6144]{1,0:T(8,128)(2,1)} %all-gather.3.cloned.1.call-done), kind=kOutput, calls=%fused_computation.1 | convolution fusion | flops 9673113600 | bytes 26738688 | tf_op jit(solution)/shard_map/dot_general | solution.py:22
  523.6 11.4 all-reduce.4.cloned.1.call-done
  535.0 832.4 %all-reduce.6.cloned.1.call-done = (bf16[1536,6144]{1,0:T(8,128)(2,1)}, bf16[6144,1536]{1,0:T(8,128)(2,1)}) async-done(((bf16[1536,6144]{1,0:T(8,128)(2,1)}, bf16[6144,1536]{1,0:T(8,128)(2,1)}), (bf16[1536,6144]{1,0:T(8,128)(2,1)}, bf16[6144,1536]{1,0:T(8,128)(2,1)})) %all-reduce.6.cloned.1.call-update) | async-done | bytes 37748752 | tf_op jit(solution)/shard_map/psum | solution.py:58
  1367.4 2.8 copy.11
  1370.2 19.2 %copy.12 = bf16[1536,6144]{1,0:T(8,128)(2,1)} copy(bf16[1536,6144]{1,0:T(8,128)(2,1)} %get-tuple-element.8) | data formatting | bytes 37748736
  1389.5 7.4 copy.13
  (19 shorter events, 0.1 us)
Async XLA Ops:
  7.2 1.9 copy-start
  7.2 134.4 %reduce-scatter.5.cloned.1.call-start = ((), (), s32[]{:S(2)}) async-start(), calls=%async_computation.3 | async-start | bytes 7864320 | tf_op jit(solution)/shard_map/reduce_scatter | solution.py:37
  27.9 1.4 copy-start.2
  28.0 227.8 %reduce-scatter.3.cloned.1.call-start = ((), (), s32[]{:S(2)}) async-start(), calls=%async_computation.2 | async-start | bytes 7864320 | tf_op jit(solution)/shard_map/reduce_scatter | solution.py:40
  44.9 331.2 %all-gather.3.cloned.1.call-start = ((), (), s32[]{:S(2)}) async-start(), calls=%async_computation.4 | async-start | bytes 7864320 | tf_op jit(solution)/shard_map/all_gather | solution.py:48
  260.0 231.7 %all-gather.5.cloned.1.call-start = ((), (), s32[]{:S(2)}) async-start(), calls=%async_computation.6 | async-start | bytes 7864320 | tf_op jit(solution)/shard_map/all_gather | solution.py:47
  260.6 274.4 %all-reduce.4.cloned.1.call-start = ((), (), s32[]{:S(2)}) async-start(), calls=%async_computation.5 | async-start | bytes 3145728 | tf_op jit(solution)/shard_map/psum | solution.py:53
  392.6 974.7 %all-reduce.6.cloned.1.call-start = ((), (), s32[]{:S(2)}) async-start(), calls=%async_computation.7 | async-start | bytes 75497472 | tf_op jit(solution)/shard_map/psum | solution.py:58
  1367.4 22.1 %slice-start = ((s8[18874368]{0:T(1024)(128)(4,1)}), s8[4194304]{0:T(1024)(128)(4,1)S(1)}, s32[]{:S(2)}) async-start(s8[18874368]{0:T(1024)(128)(4,1)} %bitcast.22), calls=%async_computation.8 | async-start | bytes 8388608
  1370.2 19.3 %slice-start.1 = ((s8[18874368]{0:T(1024)(128)(4,1)}), s8[4194304]{0:T(1024)(128)(4,1)S(1)}, s32[]{:S(2)}) async-start(s8[18874368]{0:T(1024)(128)(4,1)} %bitcast.22), calls=%async_computation.9 | async-start | bytes 8388608
  1370.2 19.3 %slice-start.2 = ((s8[18874368]{0:T(1024)(128)(4,1)}), s8[4194304]{0:T(1024)(128)(4,1)S(1)}, s32[]{:S(2)}) async-start(s8[18874368]{0:T(1024)(128)(4,1)} %bitcast.22), calls=%async_computation.10 | async-start | bytes 8388608
  1370.2 19.3 %slice-start.3 = ((s8[18874368]{0:T(1024)(128)(4,1)}), s8[4194304]{0:T(1024)(128)(4,1)S(1)}, s32[]{:S(2)}) async-start(s8[18874368]{0:T(1024)(128)(4,1)} %bitcast.22), calls=%async_computation.11 | async-start | bytes 8388608
  1370.2 19.3 %slice-start.4 = ((s8[18874368]{0:T(1024)(128)(4,1)}), s8[2097152]{0:T(1024)(128)(4,1)S(1)}, s32[]{:S(2)}) async-start(s8[18874368]{0:T(1024)(128)(4,1)} %bitcast.22), calls=%async_computation.12 | async-start | bytes 4194304
  1389.5 7.4 copy-start.1
Sparse Core Ops, SparseCore 0:
  28.1 113.4 reduce-scatter.4
  144.5 111.2 reduce-scatter.2
  260.1 115.8 all-gather.2
  378.1 113.5 all-gather.4
  493.9 41.0 all-reduce.3
  538.0 829.3 all-reduce.5
where the time goes:
time: 1400 us
  waiting for transfers between devices  1270 us (91%)
  matrix products  79.4 us (6%)
  local copies, waits for them, and re-layouts  32.8 us (2%)
  between operations  14.2 us (1%)
    psum x1, waiting for transfers between devices, per_device(): lax.psum(up_tile.astype(jnp.bfloat16), 'batch').astype(jnp.float32)  832 us
    all_gather x1, waiting for transfers between devices, per_device(): lax.all_gather(grad_share, 'fx', axis=0, tiled=True)  115 us
    reduce_scatter x1, waiting for transfers between devices, per_device(): lax.psum_scatter(back_part.astype(jnp.bfloat16), 'fx', scatter_dimension=...  114 us
    all_gather x1, waiting for transfers between devices, per_device(): lax.all_gather(act_share, 'fx', axis=0, tiled=True)  99 us
    reduce_scatter x1, waiting for transfers between devices, per_device(): lax.psum_scatter(pre_part.astype(jnp.bfloat16), 'fx', scatter_dimension=0...  96.7 us
    dot_general x2, matrix products, contract_rows(): lax.dot_general(left, right, (((0,), (0,)), ((), ())), preferred_element_...  31.9 us
    unnamed x19, local copies, waits for them, and re-layouts  31 us
  transfers between devices with their start and end apart: 6, of which 6 were waited for; matrix products, arithmetic and copies ran while one was open for 5% of the time, Pallas kernels for 0%

commit v1 on v0

v1 whole, which is shorter than its diff:
```python
import jax
import jax.numpy as jnp
from jax import lax
from jax.sharding import PartitionSpec as P

root_half = 0.7071067811865476
inv_root_tau = 0.3989422804014327
CHUNKS = 12


def gelu_value(pre_act):
    return 0.5 * pre_act * (1.0 + lax.erf(pre_act * root_half))


def gelu_slope(pre_act):
    return (
        0.5 * (1.0 + lax.erf(pre_act * root_half))
        + pre_act * jnp.exp(-0.5 * pre_act * pre_act) * inv_root_tau
    )


def contract_rows(left, right):
    return lax.dot_general(
        left, right, (((0,), (0,)), ((), ())), preferred_element_type=jnp.float32
    )


def contract_last(left, right):
    return lax.dot_general(
        left, right, (((1,), (1,)), ((), ())), preferred_element_type=jnp.float32
    )


def swap_batch(value, n_batch):
    return [
        lax.ppermute(value, "batch", [(i, (i + step) % n_batch) for i in range(n_batch)])
        for step in range(1, n_batch)
    ]


def make_per_device(n_batch, n_fx, chunks):
    half = n_fx // 2
    middle = [(half - 1, half), (half, half - 1)]

    def inward(step):
        return [(step, step + 1), (n_fx - 1 - step, n_fx - 2 - step)]

    def outward(step):
        return [(step + 1, step), (n_fx - 2 - step, n_fx - 1 - step)]

    def per_device(image_pool, escalated, up_weight, down_weight, cotangent):
        fx_width = image_pool.shape[3]
        place = lax.axis_index("fx")
        on_left = place < half
        chosen = jnp.take(image_pool[0], escalated[0], axis=0)
        inputs = chosen.reshape(-1, fx_width)
        upstream = cotangent.reshape(-1, fx_width)
        rows = inputs.shape[0]
        hidden = up_weight.shape[1]
        width = hidden // chunks

        own = jnp.stack([inputs, upstream])
        all_pairs = jnp.concatenate([own] + swap_batch(own, n_batch), axis=1)

        state = dict(
            last=None,
            sums=(
                jnp.zeros((rows, fx_width), jnp.float32),
                jnp.zeros(up_weight.shape, jnp.bfloat16),
                jnp.zeros(down_weight.shape, jnp.bfloat16),
            ),
        )

        def in_order(*values):
            if state["last"] is None:
                return values
            return lax.optimization_barrier((state["last"],) + values)[1:]

        def first_products(chunk):
            first = chunk * width
            left, right = in_order(inputs, upstream)
            part = jnp.stack([
                jnp.dot(
                    left, up_weight[:, first:first + width], preferred_element_type=jnp.float32
                ).astype(jnp.bfloat16),
                contract_last(right, down_weight[first:first + width, :]).astype(jnp.bfloat16),
            ])
            state["last"] = part
            return part

        def fold(step):
            def work(held):
                part, arrived = in_order(*held)
                part = part + arrived
                state["last"] = part
                return part

            return work

        def send_inward(step):
            return lambda part: (part, lax.ppermute(part, "fx", inward(step)))

        def send_half(part):
            low, high = part[:, :rows // 2], part[:, rows // 2:]
            kept = jnp.where(on_left, low, high)
            given = jnp.where(on_left, high, low)
            state["last"] = given
            return kept, lax.ppermute(given, "fx", middle)

        def activate(held):
            kept, arrived = in_order(*held)
            total = kept.astype(jnp.float32) + arrived.astype(jnp.float32)
            pre_act, grad_act = total[0], total[1]
            share = jnp.stack([
                gelu_value(pre_act).astype(jnp.bfloat16),
                (grad_act * gelu_slope(pre_act)).astype(jnp.bfloat16),
            ])
            state["last"] = share
            return share

        def send_share(share):
            return share, lax.ppermute(share, "fx", middle)

        def join(held):
            share, other = in_order(*held)
            full = jnp.concatenate(
                [jnp.where(on_left, share, other), jnp.where(on_left, other, share)], axis=1
            )
            state["last"] = full
            return full

        def send_outward(step):
            return lambda full: (full, lax.ppermute(full, "fx", outward(step)))

        def spread(step):
            def work(held):
                full, arrived = in_order(*held)
                takes = (place == step) | (place == n_fx - 1 - step)
                full = jnp.where(takes, arrived, full)
                state["last"] = full
                return full

            return work

        def send_replica(full):
            return [full] + swap_batch(full, n_batch)

        def last_products(chunk, held):
            first = chunk * width
            inp_sum, up_sum, down_sum = state["sums"]
            *held, pairs, inp_sum, up_sum, down_sum = in_order(
                *held, all_pairs, inp_sum, up_sum, down_sum
            )
            everyone = jnp.concatenate(held, axis=1)
            inp_sum = inp_sum + contract_last(held[0][1], up_weight[:, first:first + width])
            up_sum = lax.dynamic_update_slice(
                up_sum, contract_rows(pairs[0], everyone[1]).astype(jnp.bfloat16), (0, first)
            )
            down_sum = lax.dynamic_update_slice(
                down_sum, contract_rows(everyone[0], pairs[1]).astype(jnp.bfloat16), (first, 0)
            )
            state["sums"] = lax.optimization_barrier((inp_sum, up_sum, down_sum))
            state["last"] = state["sums"][0]

        works = [fold(step) for step in range(half - 1)] + [activate, join]
        works += [spread(step) for step in reversed(range(half - 1))]
        sends = [send_inward(step) for step in range(half - 1)] + [send_half, send_share]
        sends += [send_outward(step) for step in reversed(range(half - 1))] + [send_replica]
        depth = len(sends)
        held = {}
        for tick in range(chunks + depth):
            if tick < chunks:
                held[tick] = sends[0](first_products(tick))
            for stage, work in enumerate(works, 1):
                chunk = tick - stage
                if 0 <= chunk < chunks:
                    held[chunk] = sends[stage](work(held[chunk]))
            chunk = tick - depth
            if 0 <= chunk < chunks:
                last_products(chunk, held.pop(chunk))
        input_part, up_total, down_total = state["sums"]
        input_total = lax.psum(input_part.astype(jnp.bfloat16), "fy")
        return (input_total.reshape(cotangent.shape), up_total, down_total)

    return per_device


def solution(mesh):
    placed = (
        P("batch", None, None, "fx"),
        P("batch", None),
        P("fx", "fy"),
        P("fy", "fx"),
        P("batch", None, None, "fx"),
    )
    return jax.shard_map(
        make_per_device(mesh.shape["batch"], mesh.shape["fx"], CHUNKS),
        mesh=mesh,
        in_specs=placed,
        out_specs=(P("batch", None, None, "fx"), P("fx", "fy"), P("fy", "fx")),
        check_vma=False,
    )
```

time: 1400 us -> 586 us (0.42); the launches traced: 1400 us -> 575 us
  waiting for transfers between devices: 1270 us -> 124 us
  starting transfers between devices: 0.42 us -> 137 us
  other arithmetic: 7.44 us -> 96.5 us
  matrix products: 79.4 us -> 146 us
  local copies, waits for them, and re-layouts: 32.8 us -> 55.4 us
    psum x1 -> x0, waiting for transfers between devices: 832 us -> none  [per_device(): lax.psum(up_tile.astype(jnp.bfloat16), 'batch').astype(jnp.float32)]
    all_gather x2 -> x0, waiting for transfers between devices: 214 us -> none  [the longest x1 115 us: per_device(): lax.all_gather(grad_share, 'fx', axis=0, tiled=True)]
    reduce_scatter x2 -> x0, waiting for transfers between devices: 211 us -> none  [the longest x1 114 us: per_device(): lax.psum_scatter(back_part.astype(jnp.bfloat16), 'fx', scatter_dimension=...]
    ppermute x0 -> x61, starting transfers between devices: none -> 137 us  [the longest x12 72.8 us: send_inward(): return lambda part: (part, lax.ppermute(part, 'fx', inward(step)))]
    ppermute x0 -> x61, waiting for transfers between devices: none -> 78.4 us  [the longest x12 47.7 us: send_inward(): return lambda part: (part, lax.ppermute(part, 'fx', inward(step)))]
    dot_general x2 -> x24, matrix products: 31.9 us -> 85.7 us  [contract_rows(): lax.dot_general(left, right, (((0,), (0,)), ((), ())), preferred_element_...]
    add x0 -> x36, other arithmetic: none -> 34.4 us  [the longest x12 16.3 us: work(): part = part + arrived]
    psum x1, waiting for transfers between devices: 11.4 us -> 45.1 us  [per_device(): input_total = lax.psum(input_part.astype(jnp.bfloat16), 'fy')]
  transfers between devices with their start and end apart: 6 -> 62, of which waited for: 6 -> 14; matrix products, arithmetic and copies ran while one was open for 5% -> 47% of each run, Pallas kernels for 0% -> 0%
where the time goes in v1:
time: 586 us; the launch traced here: 575 us
  matrix products  146 us (25%)
  starting transfers between devices  137 us (23%)
  waiting for transfers between devices  124 us (21%)
  other arithmetic  96.5 us (16%)
  local copies, waits for them, and re-layouts  55.4 us (9%)
  between operations  16 us (3%)
    dot_general x24, matrix products, contract_rows(): lax.dot_general(left, right, (((0,), (0,)), ((), ())), preferred_element_...  85.7 us
    ppermute x12, starting transfers between devices, send_inward(): return lambda part: (part, lax.ppermute(part, 'fx', inward(step)))  72.8 us
    ppermute x12, waiting for transfers between devices, send_inward(): return lambda part: (part, lax.ppermute(part, 'fx', inward(step)))  47.7 us
    psum x1, waiting for transfers between devices, per_device(): input_total = lax.psum(input_part.astype(jnp.bfloat16), 'fy')  45.1 us
    dot_general x24, matrix products, contract_last(): lax.dot_general(left, right, (((1,), (1,)), ((), ())), preferred_element_...  43.3 us
    concatenate x12, local copies, waits for them, and re-layouts, last_products(): everyone = jnp.concatenate(held, axis=1)  22.3 us
    unnamed x99, local copies, waits for them, and re-layouts  17.5 us
    ppermute x12, starting transfers between devices, send_outward(): return lambda full: (full, lax.ppermute(full, 'fx', outward(step)))  17.3 us
  transfers between devices with their start and end apart: 62, of which 14 were waited for; matrix products, arithmetic and copies ran while one was open for 47% of the time, Pallas kernels for 0%

profile of v1, /device:TPU:0, one launch (start us, length us, event | category | flops | bytes accessed | tf_op | source)
XLA Modules:
  0.0 574.5 jit_solution(4090570425803214085)
XLA Ops:
  20.1 5.9 %collective-permute-start = (bf16[2,512,512]{2,1,0:T(8,128)(2,1)}, bf16[2,512,512]{2,1,0:T(8,128)(2,1)}, u32[]{:S(2)}, u32[]{:S(2)}) collective-permute-start(bf16[2,512,512]{2,1,0:T(8,128)(2,1)} %pad_maximum_fusion.2), channel_id=1, source_target_pairs={{0,4},{12,8},{1,5},{13,9},{2,6},{14,10},{3,7},{15,11},{16,20},{28,... | collective-permute-start | bytes 3145736 | tf_op jit(solution)/shard_map/ppermute | solution.py:101
  37.9 11.0 %collective-permute-done = bf16[2,512,512]{2,1,0:T(8,128)(2,1)} collective-permute-done((bf16[2,512,512]{2,1,0:T(8,128)(2,1)}, bf16[2,512,512]{2,1,0:T(8,128)(2,1)}, u32[]{:S(2)}, u32[]{:S(2)}) %collective-permute-start) | collective-permute-done | bytes 1048608 | tf_op jit(solution)/shard_map/ppermute | solution.py:101
  57.1 7.5 %collective-permute-start.3 = (bf16[2,512,512]{2,1,0:T(8,128)(2,1)S(1)}, bf16[2,512,512]{2,1,0:T(8,128)(2,1)S(1)}, u32[]{:S(2)}, u32[]{:S(2)}) collective-permute-start(bf16[2,512,512]{2,1,0:T(8,128)(2,1)S(1)} %pad_maximum_fusion.4), channel_id=1, source_target_pairs={{0,4},{12,8},{1,5},{13,9},{2,6},{14,10},{3,7},{15,11},{16,20},{28,... | collective-permute-start | bytes 3145736 | tf_op jit(solution)/shard_map/ppermute | solution.py:101
  64.5 6.8 %collective-permute-done.1 = bf16[2,512,512]{2,1,0:T(8,128)(2,1)} collective-permute-done((bf16[2,512,512]{2,1,0:T(8,128)(2,1)}, bf16[2,512,512]{2,1,0:T(8,128)(2,1)}, u32[]{:S(2)}, u32[]{:S(2)}) %collective-permute-start.1) | collective-permute-done | bytes 1048608 | tf_op jit(solution)/shard_map/ppermute | solution.py:101
  78.9 8.9 %collective-permute-start.6 = (bf16[2,512,512]{2,1,0:T(8,128)(2,1)S(1)}, bf16[2,512,512]{2,1,0:T(8,128)(2,1)S(1)}, u32[]{:S(2)}, u32[]{:S(2)}) collective-permute-start(bf16[2,512,512]{2,1,0:T(8,128)(2,1)S(1)} %pad_maximum_fusion.5), channel_id=1, source_target_pairs={{0,4},{12,8},{1,5},{13,9},{2,6},{14,10},{3,7},{15,11},{16,20},{28,... | collective-permute-start | bytes 3145736 | tf_op jit(solution)/shard_map/ppermute | solution.py:101
  87.8 5.9 %collective-permute-done.3 = bf16[2,512,512]{2,1,0:T(8,128)(2,1)S(1)} collective-permute-done((bf16[2,512,512]{2,1,0:T(8,128)(2,1)S(1)}, bf16[2,512,512]{2,1,0:T(8,128)(2,1)S(1)}, u32[]{:S(2)}, u32[]{:S(2)}) %collective-permute-start.3) | collective-permute-done | bytes 1048608 | tf_op jit(solution)/shard_map/ppermute | solution.py:101
  101.0 14.0 %collective-permute-done.6 = bf16[2,512,512]{2,1,0:T(8,128)(2,1)S(1)} collective-permute-done((bf16[2,512,512]{2,1,0:T(8,128)(2,1)S(1)}, bf16[2,512,512]{2,1,0:T(8,128)(2,1)S(1)}, u32[]{:S(2)}, u32[]{:S(2)}) %collective-permute-start.6) | collective-permute-done | bytes 1048608 | tf_op jit(solution)/shard_map/ppermute | solution.py:101
  115.0 4.4 collective-permute-start.10
  131.0 10.0 %collective-permute-done.10 = bf16[2,512,512]{2,1,0:T(8,128)(2,1)S(1)} collective-permute-done((bf16[2,512,512]{2,1,0:T(8,128)(2,1)S(1)}, bf16[2,512,512]{2,1,0:T(8,128)(2,1)S(1)}, u32[]{:S(2)}, u32[]{:S(2)}) %collective-permute-start.10) | collective-permute-done | bytes 1048608 | tf_op jit(solution)/shard_map/ppermute | solution.py:101
  143.8 5.4 collective-permute-start.16
  158.0 6.3 %collective-permute-done.14 = bf16[2,512,512]{2,1,0:T(8,128)(2,1)S(1)} collective-permute-done((bf16[2,512,512]{2,1,0:T(8,128)(2,1)S(1)}, bf16[2,512,512]{2,1,0:T(8,128)(2,1)S(1)}, u32[]{:S(2)}, u32[]{:S(2)}) %collective-permute-start.14) | collective-permute-done | bytes 1048608 | tf_op jit(solution)/shard_map/ppermute | solution.py:36
  171.1 6.7 %broadcast_in_dim.34 = bf16[1536,6144]{1,0:T(8,128)(2,1)} broadcast(bf16[]{:T(256)} %constant.17.clone.1), dimensions={} | broadcast | bytes 18874370 | tf_op jit(solution)/shard_map/broadcast_in_dim | solution.py:69
  180.8 6.6 %broadcast_in_dim.35 = bf16[6144,1536]{1,0:T(8,128)(2,1)} broadcast(bf16[]{:T(256)} %constant.17.clone.1), dimensions={} | broadcast | bytes 18874370 | tf_op jit(solution)/shard_map/broadcast_in_dim | solution.py:70
  194.0 5.4 collective-permute-start.21
  218.4 4.4 fusion.87
  230.4 6.6 %collective-permute-start.26 = (bf16[2,512,512]{2,1,0:T(8,128)(2,1)}, bf16[2,512,512]{2,1,0:T(8,128)(2,1)}, u32[]{:S(2)}, u32[]{:S(2)}) collective-permute-start(bf16[2,512,512]{2,1,0:T(8,128)(2,1)} %pad_maximum_fusion.13), channel_id=1, source_target_pairs={{0,4},{12,8},{1,5},{13,9},{2,6},{14,10},{3,7},{15,11},{16,20},{28,... | collective-permute-start | bytes 3145736 | tf_op jit(solution)/shard_map/ppermute | solution.py:101
  259.2 4.3 fusion.105
  267.2 6.6 %collective-permute-start.31 = (bf16[2,512,512]{2,1,0:T(8,128)(2,1)S(1)}, bf16[2,512,512]{2,1,0:T(8,128)(2,1)}, u32[]{:S(2)}, u32[]{:S(2)}) collective-permute-start(bf16[2,512,512]{2,1,0:T(8,128)(2,1)S(1)} %pad_maximum_fusion.15), channel_id=1, source_target_pairs={{0,4},{12,8},{1,5},{13,9},{2,6},{14,10},{3,7},{15,11},{16,20},{28,... | collective-permute-start | bytes 3145736 | tf_op jit(solution)/shard_map/ppermute | solution.py:101
  292.4 4.3 fusion.111
  304.4 6.7 %collective-permute-start.36 = (bf16[2,512,512]{2,1,0:T(8,128)(2,1)}, bf16[2,512,512]{2,1,0:T(8,128)(2,1)}, u32[]{:S(2)}, u32[]{:S(2)}) collective-permute-start(bf16[2,512,512]{2,1,0:T(8,128)(2,1)} %pad_maximum_fusion.17), channel_id=1, source_target_pairs={{0,4},{12,8},{1,5},{13,9},{2,6},{14,10},{3,7},{15,11},{16,20},{28,... | collective-permute-start | bytes 3145736 | tf_op jit(solution)/shard_map/ppermute | solution.py:101
  329.7 4.4 fusion.123
  340.7 6.5 %collective-permute-start.41 = (bf16[2,512,512]{2,1,0:T(8,128)(2,1)S(1)}, bf16[2,512,512]{2,1,0:T(8,128)(2,1)}, u32[]{:S(2)}, u32[]{:S(2)}) collective-permute-start(bf16[2,512,512]{2,1,0:T(8,128)(2,1)S(1)} %pad_maximum_fusion.19), channel_id=1, source_target_pairs={{0,4},{12,8},{1,5},{13,9},{2,6},{14,10},{3,7},{15,11},{16,20},{28,... | collective-permute-start | bytes 3145736 | tf_op jit(solution)/shard_map/ppermute | solution.py:101
  365.3 4.3 fusion.135
  376.2 6.7 %collective-permute-start.46 = (bf16[2,512,512]{2,1,0:T(8,128)(2,1)S(1)}, bf16[2,512,512]{2,1,0:T(8,128)(2,1)}, u32[]{:S(2)}, u32[]{:S(2)}) collective-permute-start(bf16[2,512,512]{2,1,0:T(8,128)(2,1)S(1)} %pad_maximum_fusion.21), channel_id=1, source_target_pairs={{0,4},{12,8},{1,5},{13,9},{2,6},{14,10},{3,7},{15,11},{16,20},{28,... | collective-permute-start | bytes 3145736 | tf_op jit(solution)/shard_map/ppermute | solution.py:101
  401.6 4.2 fusion.147
  427.3 4.3 fusion.165
  459.1 12.5 %collective-permute-done.56 = bf16[2,512,512]{2,1,0:T(8,128)(2,1)} collective-permute-done((bf16[2,512,512]{2,1,0:T(8,128)(2,1)}, bf16[2,512,512]{2,1,0:T(8,128)(2,1)}, u32[]{:S(2)}, u32[]{:S(2)}) %collective-permute-start.56) | collective-permute-done | bytes 1048608 | tf_op jit(solution)/shard_map/ppermute | solution.py:133
  482.8 4.2 fusion.183
  497.2 4.2 fusion.201
  501.4 4.2 fusion.195
  505.6 5.2 collective-permute-done.59
  519.5 45.1 %all-reduce.2.cloned.1.call-done = bf16[1,2,256,1536]{3,2,1,0:T(8,128)(2,1)} async-done(((bf16[1,2,256,1536]{3,2,1,0:T(8,128)(2,1)}), bf16[1,2,256,1536]{3,2,1,0:T(8,128)(2,1)}) %all-reduce.2.cloned.1.call-update) | async-done | bytes 1572880 | tf_op jit(solution)/shard_map/psum | solution.py:182
  (398 shorter events, 315.1 us)
Async XLA Ops:
  7.2 557.5 %all-reduce.2.cloned.1.call-start = ((), (), s32[]{:S(2)}) async-start(), calls=%async_computation | async-start | bytes 3145728 | tf_op jit(solution)/shard_map/psum | solution.py:182
  31.9 39.4 %collective-permute-start.1 = (bf16[2,512,512]{2,1,0:T(8,128)(2,1)}, bf16[2,512,512]{2,1,0:T(8,128)(2,1)}, u32[]{:S(2)}, u32[]{:S(2)}) collective-permute-start(bf16[2,512,512]{2,1,0:T(8,128)(2,1)} %pad_maximum_fusion.3), channel_id=1, source_target_pairs={{0,4},{12,8},{1,5},{13,9},{2,6},{14,10},{3,7},{15,11},{16,20},{28,... | collective-permute-start | bytes 3145736 | tf_op jit(solution)/shard_map/ppermute | solution.py:101
  36.3 115.9 %collective-permute-start.15 = (bf16[2,512,1536]{2,1,0:T(8,128)(2,1)}, bf16[2,512,1536]{2,1,0:T(8,128)(2,1)}, u32[]{:S(2)}, u32[]{:S(2)}) collective-permute-start(bf16[2,512,1536]{2,1,0:T(8,128)(2,1)} %pad_maximum_fusion.1), channel_id=1, source_target_pairs={{0,16},{16,0},{1,17},{17,1},{2,18},{18,2},{3,19},{19,3},{4,20},{20... | collective-permute-start | bytes 9437192 | tf_op jit(solution)/shard_map/ppermute | solution.py:36
  57.1 36.6 %collective-permute-start.3 = (bf16[2,512,512]{2,1,0:T(8,128)(2,1)S(1)}, bf16[2,512,512]{2,1,0:T(8,128)(2,1)S(1)}, u32[]{:S(2)}, u32[]{:S(2)}) collective-permute-start(bf16[2,512,512]{2,1,0:T(8,128)(2,1)S(1)} %pad_maximum_fusion.4), channel_id=1, source_target_pairs={{0,4},{12,8},{1,5},{13,9},{2,6},{14,10},{3,7},{15,11},{16,20},{28,... | collective-permute-start | bytes 3145736 | tf_op jit(solution)/shard_map/ppermute | solution.py:101
  78.9 36.1 %collective-permute-start.6 = (bf16[2,512,512]{2,1,0:T(8,128)(2,1)S(1)}, bf16[2,512,512]{2,1,0:T(8,128)(2,1)S(1)}, u32[]{:S(2)}, u32[]{:S(2)}) collective-permute-start(bf16[2,512,512]{2,1,0:T(8,128)(2,1)S(1)} %pad_maximum_fusion.5), channel_id=1, source_target_pairs={{0,4},{12,8},{1,5},{13,9},{2,6},{14,10},{3,7},{15,11},{16,20},{28,... | collective-permute-start | bytes 3145736 | tf_op jit(solution)/shard_map/ppermute | solution.py:101
  143.8 50.3 %collective-permute-start.16 = (bf16[2,512,512]{2,1,0:T(8,128)(2,1)}, bf16[2,512,512]{2,1,0:T(8,128)(2,1)}, u32[]{:S(2)}, u32[]{:S(2)}) collective-permute-start(bf16[2,512,512]{2,1,0:T(8,128)(2,1)} %pad_maximum_fusion.9), channel_id=1, source_target_pairs={{0,4},{12,8},{1,5},{13,9},{2,6},{14,10},{3,7},{15,11},{16,20},{28,... | collective-permute-start | bytes 3145736 | tf_op jit(solution)/shard_map/ppermute | solution.py:101
  149.6 52.7 %collective-permute-start.17 = (bf16[2,256,512]{2,1,0:T(8,128)(2,1)}, bf16[2,256,512]{2,1,0:T(8,128)(2,1)}, u32[]{:S(2)}, u32[]{:S(2)}) collective-permute-start(bf16[2,256,512]{2,1,0:T(8,128)(2,1)} %get-tuple-element.504), channel_id=1, source_target_pairs={{4,8},{8,4},{5,9},{9,5},{6,10},{10,6},{7,11},{11,7},{20,24},{24,20... | collective-permute-start | bytes 1572872 | tf_op jit(solution)/shard_map/ppermute | solution.py:108
  152.2 53.9 %collective-permute-start.18 = (bf16[2,256,512]{2,1,0:T(8,128)(2,1)S(1)}, bf16[2,256,512]{2,1,0:T(8,128)(2,1)}, u32[]{:S(2)}, u32[]{:S(2)}) collective-permute-start(bf16[2,256,512]{2,1,0:T(8,128)(2,1)S(1)} %pad_maximum_fusion.29), channel_id=1, source_target_pairs={{4,8},{8,4},{5,9},{9,5},{6,10},{10,6},{7,11},{11,7},{20,24},{24,20... | collective-permute-start | bytes 1572872 | tf_op jit(solution)/shard_map/ppermute | solution.py:122
  156.5 53.3 %collective-permute-start.19 = (bf16[2,512,512]{2,1,0:T(8,128)(2,1)}, bf16[2,512,512]{2,1,0:T(8,128)(2,1)}, u32[]{:S(2)}, u32[]{:S(2)}) collective-permute-start(bf16[2,512,512]{2,1,0:T(8,128)(2,1)} %pad_maximum_fusion.10), channel_id=1, source_target_pairs={{4,0},{8,12},{5,1},{9,13},{6,2},{10,14},{7,3},{11,15},{20,16},{24,... | collective-permute-start | bytes 3145736 | tf_op jit(solution)/shard_map/ppermute | solution.py:133
  164.2 48.6 %collective-permute-start.20 = (bf16[2,512,512]{2,1,0:T(8,128)(2,1)S(1)}, bf16[2,512,512]{2,1,0:T(8,128)(2,1)}, u32[]{:S(2)}, u32[]{:S(2)}) collective-permute-start(bf16[2,512,512]{2,1,0:T(8,128)(2,1)S(1)} %broadcast_select_fusion.10), channel_id=1, source_target_pairs={{0,16},{16,0},{1,17},{17,1},{2,18},{18,2},{3,19},{19,3},{4,20},{20... | collective-permute-start | bytes 3145736 | tf_op jit(solution)/shard_map/ppermute | solution.py:36
  194.0 36.3 %collective-permute-start.21 = (bf16[2,512,512]{2,1,0:T(8,128)(2,1)S(1)}, bf16[2,512,512]{2,1,0:T(8,128)(2,1)}, u32[]{:S(2)}, u32[]{:S(2)}) collective-permute-start(bf16[2,512,512]{2,1,0:T(8,128)(2,1)S(1)} %pad_maximum_fusion.11), channel_id=1, source_target_pairs={{0,4},{12,8},{1,5},{13,9},{2,6},{14,10},{3,7},{15,11},{16,20},{28,... | collective-permute-start | bytes 3145736 | tf_op jit(solution)/shard_map/ppermute | solution.py:101
  202.4 37.2 %collective-permute-start.22 = (bf16[2,256,512]{2,1,0:T(8,128)(2,1)}, bf16[2,256,512]{2,1,0:T(8,128)(2,1)}, u32[]{:S(2)}, u32[]{:S(2)}) collective-permute-start(bf16[2,256,512]{2,1,0:T(8,128)(2,1)} %get-tuple-element.498), channel_id=1, source_target_pairs={{4,8},{8,4},{5,9},{9,5},{6,10},{10,6},{7,11},{11,7},{20,24},{24,20... | collective-permute-start | bytes 1572872 | tf_op jit(solution)/shard_map/ppermute | solution.py:108
  206.2 34.9 %collective-permute-start.23 = (bf16[2,256,512]{2,1,0:T(8,128)(2,1)}, bf16[2,256,512]{2,1,0:T(8,128)(2,1)}, u32[]{:S(2)}, u32[]{:S(2)}) collective-permute-start(bf16[2,256,512]{2,1,0:T(8,128)(2,1)} %pad_maximum_fusion.30), channel_id=1, source_target_pairs={{4,8},{8,4},{5,9},{9,5},{6,10},{10,6},{7,11},{11,7},{20,24},{24,20... | collective-permute-start | bytes 1572872 | tf_op jit(solution)/shard_map/ppermute | solution.py:122
  209.8 33.6 %collective-permute-start.24 = (bf16[2,512,512]{2,1,0:T(8,128)(2,1)}, bf16[2,512,512]{2,1,0:T(8,128)(2,1)}, u32[]{:S(2)}, u32[]{:S(2)}) collective-permute-start(bf16[2,512,512]{2,1,0:T(8,128)(2,1)} %pad_maximum_fusion.12), channel_id=1, source_target_pairs={{4,0},{8,12},{5,1},{9,13},{6,2},{10,14},{7,3},{11,15},{20,16},{24,... | collective-permute-start | bytes 3145736 | tf_op jit(solution)/shard_map/ppermute | solution.py:133
  230.4 36.8 %collective-permute-start.26 = (bf16[2,512,512]{2,1,0:T(8,128)(2,1)}, bf16[2,512,512]{2,1,0:T(8,128)(2,1)}, u32[]{:S(2)}, u32[]{:S(2)}) collective-permute-start(bf16[2,512,512]{2,1,0:T(8,128)(2,1)} %pad_maximum_fusion.13), channel_id=1, source_target_pairs={{0,4},{12,8},{1,5},{13,9},{2,6},{14,10},{3,7},{15,11},{16,20},{28,... | collective-permute-start | bytes 3145736 | tf_op jit(solution)/shard_map/ppermute | solution.py:101
  249.9 34.2 %collective-permute-start.29 = (bf16[2,512,512]{2,1,0:T(8,128)(2,1)}, bf16[2,512,512]{2,1,0:T(8,128)(2,1)}, u32[]{:S(2)}, u32[]{:S(2)}) collective-permute-start(bf16[2,512,512]{2,1,0:T(8,128)(2,1)} %pad_maximum_fusion.14), channel_id=1, source_target_pairs={{4,0},{8,12},{5,1},{9,13},{6,2},{10,14},{7,3},{11,15},{20,16},{24,... | collective-permute-start | bytes 3145736 | tf_op jit(solution)/shard_map/ppermute | solution.py:133
  251.4 35.6 %collective-permute-start.30 = (bf16[2,512,512]{2,1,0:T(8,128)(2,1)S(1)}, bf16[2,512,512]{2,1,0:T(8,128)(2,1)}, u32[]{:S(2)}, u32[]{:S(2)}) collective-permute-start(bf16[2,512,512]{2,1,0:T(8,128)(2,1)S(1)} %broadcast_select_fusion.8), channel_id=1, source_target_pairs={{0,16},{16,0},{1,17},{17,1},{2,18},{18,2},{3,19},{19,3},{4,20},{20... | collective-permute-start | bytes 3145736 | tf_op jit(solution)/shard_map/ppermute | solution.py:36
  267.2 37.2 %collective-permute-start.31 = (bf16[2,512,512]{2,1,0:T(8,128)(2,1)S(1)}, bf16[2,512,512]{2,1,0:T(8,128)(2,1)}, u32[]{:S(2)}, u32[]{:S(2)}) collective-permute-start(bf16[2,512,512]{2,1,0:T(8,128)(2,1)S(1)} %pad_maximum_fusion.15), channel_id=1, source_target_pairs={{0,4},{12,8},{1,5},{13,9},{2,6},{14,10},{3,7},{15,11},{16,20},{28,... | collective-permute-start | bytes 3145736 | tf_op jit(solution)/shard_map/ppermute | solution.py:101
  276.7 36.8 %collective-permute-start.32 = (bf16[2,256,512]{2,1,0:T(8,128)(2,1)}, bf16[2,256,512]{2,1,0:T(8,128)(2,1)}, u32[]{:S(2)}, u32[]{:S(2)}) collective-permute-start(bf16[2,256,512]{2,1,0:T(8,128)(2,1)} %get-tuple-element.486), channel_id=1, source_target_pairs={{4,8},{8,4},{5,9},{9,5},{6,10},{10,6},{7,11},{11,7},{20,24},{24,20... | collective-permute-start | bytes 1572872 | tf_op jit(solution)/shard_map/ppermute | solution.py:108
  280.5 36.0 %collective-permute-start.33 = (bf16[2,256,512]{2,1,0:T(8,128)(2,1)}, bf16[2,256,512]{2,1,0:T(8,128)(2,1)}, u32[]{:S(2)}, u32[]{:S(2)}) collective-permute-start(bf16[2,256,512]{2,1,0:T(8,128)(2,1)} %pad_maximum_fusion.32), channel_id=1, source_target_pairs={{4,8},{8,4},{5,9},{9,5},{6,10},{10,6},{7,11},{11,7},{20,24},{24,20... | collective-permute-start | bytes 1572872 | tf_op jit(solution)/shard_map/ppermute | solution.py:122
  284.1 36.1 %collective-permute-start.34 = (bf16[2,512,512]{2,1,0:T(8,128)(2,1)}, bf16[2,512,512]{2,1,0:T(8,128)(2,1)}, u32[]{:S(2)}, u32[]{:S(2)}) collective-permute-start(bf16[2,512,512]{2,1,0:T(8,128)(2,1)} %pad_maximum_fusion.16), channel_id=1, source_target_pairs={{4,0},{8,12},{5,1},{9,13},{6,2},{10,14},{7,3},{11,15},{20,16},{24,... | collective-permute-start | bytes 3145736 | tf_op jit(solution)/shard_map/ppermute | solution.py:133
  289.1 34.1 %collective-permute-start.35 = (bf16[2,512,512]{2,1,0:T(8,128)(2,1)S(1)}, bf16[2,512,512]{2,1,0:T(8,128)(2,1)S(1)}, u32[]{:S(2)}, u32[]{:S(2)}) collective-permute-start(bf16[2,512,512]{2,1,0:T(8,128)(2,1)S(1)} %broadcast_select_fusion.7), channel_id=1, source_target_pairs={{0,16},{16,0},{1,17},{17,1},{2,18},{18,2},{3,19},{19,3},{4,20},{20... | collective-permute-start | bytes 3145736 | tf_op jit(solution)/shard_map/ppermute | solution.py:36
  304.4 36.3 %collective-permute-start.36 = (bf16[2,512,512]{2,1,0:T(8,128)(2,1)}, bf16[2,512,512]{2,1,0:T(8,128)(2,1)}, u32[]{:S(2)}, u32[]{:S(2)}) collective-permute-start(bf16[2,512,512]{2,1,0:T(8,128)(2,1)} %pad_maximum_fusion.17), channel_id=1, source_target_pairs={{0,4},{12,8},{1,5},{13,9},{2,6},{14,10},{3,7},{15,11},{16,20},{28,... | collective-permute-start | bytes 3145736 | tf_op jit(solution)/shard_map/ppermute | solution.py:101
  313.5 36.6 %collective-permute-start.37 = (bf16[2,256,512]{2,1,0:T(8,128)(2,1)}, bf16[2,256,512]{2,1,0:T(8,128)(2,1)}, u32[]{:S(2)}, u32[]{:S(2)}) collective-permute-start(bf16[2,256,512]{2,1,0:T(8,128)(2,1)} %get-tuple-element.480), channel_id=1, source_target_pairs={{4,8},{8,4},{5,9},{9,5},{6,10},{10,6},{7,11},{11,7},{20,24},{24,20... | collective-permute-start | bytes 1572872 | tf_op jit(solution)/shard_map/ppermute | solution.py:108
  316.5 37.5 %collective-permute-start.38 = (bf16[2,256,512]{2,1,0:T(8,128)(2,1)S(1)}, bf16[2,256,512]{2,1,0:T(8,128)(2,1)}, u32[]{:S(2)}, u32[]{:S(2)}) collective-permute-start(bf16[2,256,512]{2,1,0:T(8,128)(2,1)S(1)} %pad_maximum_fusion.33), channel_id=1, source_target_pairs={{4,8},{8,4},{5,9},{9,5},{6,10},{10,6},{7,11},{11,7},{20,24},{24,20... | collective-permute-start | bytes 1572872 | tf_op jit(solution)/shard_map/ppermute | solution.py:122
  320.2 36.3 %collective-permute-start.39 = (bf16[2,512,512]{2,1,0:T(8,128)(2,1)}, bf16[2,512,512]{2,1,0:T(8,128)(2,1)}, u32[]{:S(2)}, u32[]{:S(2)}) collective-permute-start(bf16[2,512,512]{2,1,0:T(8,128)(2,1)} %pad_maximum_fusion.18), channel_id=1, source_target_pairs={{4,0},{8,12},{5,1},{9,13},{6,2},{10,14},{7,3},{11,15},{20,16},{24,... | collective-permute-start | bytes 3145736 | tf_op jit(solution)/shard_map/ppermute | solution.py:133
  323.2 36.5 %collective-permute-start.40 = (bf16[2,512,512]{2,1,0:T(8,128)(2,1)S(1)}, bf16[2,512,512]{2,1,0:T(8,128)(2,1)}, u32[]{:S(2)}, u32[]{:S(2)}) collective-permute-start(bf16[2,512,512]{2,1,0:T(8,128)(2,1)S(1)} %broadcast_select_fusion.6), channel_id=1, source_target_pairs={{0,16},{16,0},{1,17},{17,1},{2,18},{18,2},{3,19},{19,3},{4,20},{20... | collective-permute-start | bytes 3145736 | tf_op jit(solution)/shard_map/ppermute | solution.py:36
  340.7 35.5 %collective-permute-start.41 = (bf16[2,512,512]{2,1,0:T(8,128)(2,1)S(1)}, bf16[2,512,512]{2,1,0:T(8,128)(2,1)}, u32[]{:S(2)}, u32[]{:S(2)}) collective-permute-start(bf16[2,512,512]{2,1,0:T(8,128)(2,1)S(1)} %pad_maximum_fusion.19), channel_id=1, source_target_pairs={{0,4},{12,8},{1,5},{13,9},{2,6},{14,10},{3,7},{15,11},{16,20},{28,... | collective-permute-start | bytes 3145736 | tf_op jit(solution)/shard_map/ppermute | solution.py:101
  350.1 35.4 %collective-permute-start.42 = (bf16[2,256,512]{2,1,0:T(8,128)(2,1)}, bf16[2,256,512]{2,1,0:T(8,128)(2,1)}, u32[]{:S(2)}, u32[]{:S(2)}) collective-permute-start(bf16[2,256,512]{2,1,0:T(8,128)(2,1)} %get-tuple-element.474), channel_id=1, source_target_pairs={{4,8},{8,4},{5,9},{9,5},{6,10},{10,6},{7,11},{11,7},{20,24},{24,20... | collective-permute-start | bytes 1572872 | tf_op jit(solution)/shard_map/ppermute | solution.py:108
  353.9 33.1 %collective-permute-start.43 = (bf16[2,256,512]{2,1,0:T(8,128)(2,1)}, bf16[2,256,512]{2,1,0:T(8,128)(2,1)}, u32[]{:S(2)}, u32[]{:S(2)}) collective-permute-start(bf16[2,256,512]{2,1,0:T(8,128)(2,1)} %pad_maximum_fusion.34), channel_id=1, source_target_pairs={{4,8},{8,4},{5,9},{9,5},{6,10},{10,6},{7,11},{11,7},{20,24},{24,20... | collective-permute-start | bytes 1572872 | tf_op jit(solution)/shard_map/ppermute | solution.py:122
  356.6 32.8 %collective-permute-start.44 = (bf16[2,512,512]{2,1,0:T(8,128)(2,1)S(1)}, bf16[2,512,512]{2,1,0:T(8,128)(2,1)}, u32[]{:S(2)}, u32[]{:S(2)}) collective-permute-start(bf16[2,512,512]{2,1,0:T(8,128)(2,1)S(1)} %pad_maximum_fusion.20), channel_id=1, source_target_pairs={{4,0},{8,12},{5,1},{9,13},{6,2},{10,14},{7,3},{11,15},{20,16},{24,... | collective-permute-start | bytes 3145736 | tf_op jit(solution)/shard_map/ppermute | solution.py:133
  376.2 33.8 %collective-permute-start.46 = (bf16[2,512,512]{2,1,0:T(8,128)(2,1)S(1)}, bf16[2,512,512]{2,1,0:T(8,128)(2,1)}, u32[]{:S(2)}, u32[]{:S(2)}) collective-permute-start(bf16[2,512,512]{2,1,0:T(8,128)(2,1)S(1)} %pad_maximum_fusion.21), channel_id=1, source_target_pairs={{0,4},{12,8},{1,5},{13,9},{2,6},{14,10},{3,7},{15,11},{16,20},{28,... | collective-permute-start | bytes 3145736 | tf_op jit(solution)/shard_map/ppermute | solution.py:101
  (73 other events, 1101.0 us)
Sparse Core Ops, SparseCore 0:
  519.6 44.9 all-reduce.1
